TPU v7x, 32 devices: a whole 2x2x4 slice. The times are simulated.
32 devices in a mesh: dp: 16 (over z, x, core), tp: 2 (over y).
Axes of the slice: x: 2, y: 2, z: 4, core: 2. Of those that a mesh axis runs over, the one named last changes fastest.
Arguments:
- layer_in: float32 [75264, 512], P(('dp', 'tp')), may hold values from -6 to 6
- out_grad: float32 [75264, 512], P(('dp', 'tp')), may hold values from -6 to 6
- w_qkv: bfloat16 [512, 1536], P('dp', 'tp'), may hold values from -0.25 to 0.25
- b_qv: bfloat16 [1024], P('dp'), may hold values from -3 to 3
- w_proj: bfloat16 [512, 512], P('tp', 'dp'), may hold values from -1 to 1
- b_proj: bfloat16 [512], P('dp'), may hold values from -3 to 3
- w_fc1: bfloat16 [512, 2048], P('dp', 'tp'), may hold values from -0.25 to 0.25
- b_fc1: bfloat16 [2048], P('dp'), may hold values from -3 to 3
- w_fc2: bfloat16 [2048, 512], P('tp', 'dp'), may hold values from -0.25 to 0.25
- b_fc2: bfloat16 [512], P('dp'), may hold values from -3 to 3
- gain_one: bfloat16 [512], P('dp'), may hold values from 0.099609375 to 1.8984375
- shift_one: bfloat16 [512], P('dp'), may hold values from -3 to 3
- gain_two: bfloat16 [512], P('dp'), may hold values from 0.099609375 to 1.8984375
- shift_two: bfloat16 [512], P('dp'), may hold values from -3 to 3
- rel_table: bfloat16 [16, 169], replicated, may hold values from -4 to 4
- rel_index: int32 [49, 49], replicated, may hold values from 0 to 168, as said below
Outputs:
- layer_out: float32 [75264, 512], P(('dp', 'tp'))
- in_grad: float32 [75264, 512], P(('dp', 'tp'))
- grad_w_qkv: float32 [512, 1536], P('dp', 'tp')
- grad_b_qv: float32 [1024], P('dp')
- grad_w_proj: float32 [512, 512], P('tp', 'dp')
- grad_b_proj: float32 [512], P('dp')
- grad_w_fc1: float32 [512, 2048], P('dp', 'tp')
- grad_b_fc1: float32 [2048], P('dp')
- grad_w_fc2: float32 [2048, 512], P('tp', 'dp')
- grad_b_fc2: float32 [512], P('dp')
- grad_gain_one: float32 [512], P('dp')
- grad_shift_one: float32 [512], P('dp')
- grad_gain_two: float32 [512], P('dp')
- grad_shift_two: float32 [512], P('dp')
- grad_rel_table: float32 [16, 169], replicated
Inputs may be any that keep to these rules, and one draw needn't show every extreme that they name: `rel_index`: entry [i, j] depends only on the row offset and the column offset between place i and place j of a 7 x 7 window, and different offset pairs have different entries.
All inputs are finite; a program needn't handle non-finite values.
Results may differ from a plain program's by a relative error of at most 0.017.
Values may be sent and summed in bfloat16 or wider, within the bound.
A program may use at most 320 MiB of HBM per device.

v0:
```python
import jax
import jax.numpy as jnp
from jax import lax
from jax.sharding import PartitionSpec as P

D = 512
HEADS = 16
HEAD_DIM = 32
RES = 14
WIN = 7
SHIFT = 3
TBL = 169


HIGHEST = lax.Precision.HIGHEST


def layer_norm(tensor, gain, shift):
    average = jnp.mean(tensor, axis=-1, keepdims=True)
    centred = tensor - average
    spread = jnp.mean(centred * centred, axis=-1, keepdims=True)
    return centred * lax.rsqrt(spread + 1e-05) * gain + shift


def to_windows(tensor, images):
    per_side = RES // WIN
    inner = tensor.shape[1:]
    lattice = tensor.reshape((images, RES, RES) + inner)
    lattice = jnp.roll(lattice, (-SHIFT, -SHIFT), axis=(1, 2))
    lattice = lattice.reshape((images, per_side, WIN, per_side, WIN) + inner)
    lattice = jnp.swapaxes(lattice, 2, 3)
    return lattice.reshape((images * per_side * per_side, WIN * WIN) + inner)


def from_windows(tensor, images):
    per_side = RES // WIN
    inner = tensor.shape[2:]
    lattice = tensor.reshape((images, per_side, per_side, WIN, WIN) + inner)
    lattice = jnp.swapaxes(lattice, 2, 3).reshape((images, RES, RES) + inner)
    lattice = jnp.roll(lattice, (SHIFT, SHIFT), axis=(1, 2))
    return lattice.reshape((images * RES * RES,) + inner)


def window_masks():
    per_side = RES // WIN
    places = jnp.arange(RES, dtype=jnp.int32)
    band_of = (places >= RES - WIN).astype(jnp.int32) + (places >= RES - SHIFT).astype(jnp.int32)
    labels = band_of[:, None] * 3 + band_of[None, :]
    labels = labels.reshape(per_side, WIN, per_side, WIN)
    labels = jnp.swapaxes(labels, 1, 2).reshape(per_side * per_side, WIN * WIN)
    return jnp.where(labels[:, :, None] != labels[:, None, :], -100.0, 0.0).astype(jnp.float32)


def window_scores(query_win, key_win, offsets, masks, images):
    per_image = (RES // WIN) ** 2
    scores = jnp.einsum(
        "wqhd,wkhd->whqk", query_win, key_win, preferred_element_type=jnp.float32
    ) * HEAD_DIM ** (-0.5)
    shaped = (
        scores.reshape((images, per_image) + scores.shape[1:])
        + offsets[None, None]
        + masks[None, :, None]
    )
    return shaped.reshape(scores.shape)


def contract_rows(left, right):
    return lax.dot_general(
        left, right, (((0,), (0,)), ((), ())), preferred_element_type=jnp.float32
    )


def contract_cols(left, right):
    return lax.dot_general(
        left, right, (((1,), (1,)), ((), ())), preferred_element_type=jnp.float32
    )


def gelu_exact(tensor):
    return jax.nn.gelu(tensor, approximate=False)


def gelu_back(hidden, upstream):
    _, pullback = jax.vjp(gelu_exact, hidden)
    return pullback(upstream)[0]


def place_part(piece, length, start):
    return lax.dynamic_update_slice_in_dim(
        jnp.zeros((length,) + piece.shape[1:], jnp.float32), piece, start, 0
    )


def per_device(
    layer_in,
    out_grad,
    w_qkv,
    b_qv,
    w_proj,
    b_proj,
    w_fc1,
    b_fc1,
    w_fc2,
    b_fc2,
    gain_one,
    shift_one,
    gain_two,
    shift_two,
    rel_table,
    rel_index,
):
    rows = layer_in.shape[0]
    tp_size = lax.axis_size("tp")
    tp_here = lax.axis_index("tp")
    dp_size = lax.axis_size("dp")
    dp_here = lax.axis_index("dp")
    scale = HEAD_DIM ** (-0.5)
    gathered = (
        lax.all_gather(w_qkv, "dp", axis=0, tiled=True),
        lax.all_gather(w_proj, "dp", axis=1, tiled=True),
        lax.all_gather(w_fc1, "dp", axis=0, tiled=True),
        lax.all_gather(w_fc2, "dp", axis=1, tiled=True),
        lax.all_gather(b_qv, "dp", axis=0, tiled=True),
        lax.all_gather(b_proj, "dp", axis=0, tiled=True),
        lax.all_gather(b_fc1, "dp", axis=0, tiled=True),
        lax.all_gather(b_fc2, "dp", axis=0, tiled=True),
        lax.all_gather(gain_one, "dp", axis=0, tiled=True),
        lax.all_gather(shift_one, "dp", axis=0, tiled=True),
        lax.all_gather(gain_two, "dp", axis=0, tiled=True),
        lax.all_gather(shift_two, "dp", axis=0, tiled=True),
    )
    qkv_full, proj_full, fc1_full, fc2_full = (gathered[0], gathered[1], gathered[2], gathered[3])
    bias_qv, bias_proj, bias_fc1, bias_fc2, gain_a, shift_a, gain_b, shift_b = [
        vector.astype(jnp.float32) for vector in gathered[4:]
    ]
    normed = layer_norm(layer_in, gain_a, shift_a).astype(jnp.bfloat16)
    heads_now = HEADS // tp_size
    head_start = tp_here * heads_now
    attn_images = tp_size * rows // (RES * RES)
    qkv_use, proj_use = (qkv_full, proj_full)
    normed_use = lax.all_gather(normed, "tp", axis=0, tiled=True)
    qv_mine = lax.dynamic_slice_in_dim(
        bias_qv, head_start * 2 * HEAD_DIM, heads_now * 2 * HEAD_DIM
    ).reshape(heads_now, 2, HEAD_DIM)
    table_mine = lax.dynamic_slice_in_dim(rel_table.astype(jnp.float32), head_start, heads_now, 0)
    onehot = (rel_index.reshape(-1)[:, None] == jnp.arange(TBL, dtype=jnp.int32)[None, :]).astype(
        jnp.float32
    )
    offsets = jnp.dot(table_mine, onehot.T, precision=HIGHEST).reshape(
        heads_now, WIN * WIN, WIN * WIN
    )
    masks = window_masks()
    project = jnp.dot(normed_use, qkv_use, preferred_element_type=jnp.float32).reshape(
        -1, heads_now, 3, HEAD_DIM
    )
    query_win = to_windows((project[:, :, 0] + qv_mine[:, 0]).astype(jnp.bfloat16), attn_images)
    key_win = to_windows(project[:, :, 1].astype(jnp.bfloat16), attn_images)
    value_win = to_windows((project[:, :, 2] + qv_mine[:, 1]).astype(jnp.bfloat16), attn_images)
    scores = window_scores(query_win, key_win, offsets, masks, attn_images)
    row_peak = jnp.max(scores, axis=-1, keepdims=True)
    log_total = row_peak + jnp.log(jnp.sum(jnp.exp(scores - row_peak), axis=-1, keepdims=True))
    probs_low = jnp.exp(scores - log_total).astype(jnp.bfloat16)
    mixed_win = jnp.einsum(
        "whqk,wkhd->wqhd", probs_low, value_win, preferred_element_type=jnp.float32
    )
    mixed = (
        from_windows(mixed_win, attn_images).reshape(-1, heads_now * HEAD_DIM).astype(jnp.bfloat16)
    )
    attn_out = lax.psum_scatter(
        jnp.dot(mixed, proj_use, preferred_element_type=jnp.float32).astype(jnp.bfloat16),
        "tp",
        scatter_dimension=0,
        tiled=True,
    ).astype(jnp.float32)
    middle = layer_in + attn_out + bias_proj
    normed_two = layer_norm(middle, gain_b, shift_b).astype(jnp.bfloat16)
    fc1_all, fc2_all = (
        lax.all_gather(fc1_full, "tp", axis=1, tiled=True),
        lax.all_gather(fc2_full, "tp", axis=0, tiled=True),
    )
    hidden = jnp.dot(normed_two, fc1_all, preferred_element_type=jnp.float32) + bias_fc1
    active = gelu_exact(hidden).astype(jnp.bfloat16)
    mlp_out = jnp.dot(active, fc2_all, preferred_element_type=jnp.float32)
    layer_out = middle + mlp_out + bias_fc2
    qkv_full, proj_full, fc1_full, fc2_full = (
        lax.all_gather(w_qkv, "dp", axis=0, tiled=True),
        lax.all_gather(w_proj, "dp", axis=1, tiled=True),
        lax.all_gather(w_fc1, "dp", axis=0, tiled=True),
        lax.all_gather(w_fc2, "dp", axis=1, tiled=True),
    )
    qkv_use, proj_use = (qkv_full, proj_full)
    out_low = out_grad.astype(jnp.bfloat16)
    fc2_bias_grad = jnp.sum(out_grad, axis=0)
    fc2_whole = contract_rows(active, out_low)
    hidden_grad = gelu_back(hidden, contract_cols(out_low, fc2_all)).astype(jnp.bfloat16)
    fc1_whole = contract_rows(normed_two, hidden_grad)
    fc1_bias_grad = jnp.sum(hidden_grad, axis=0, dtype=jnp.float32)
    fc1_wgrad, fc2_wgrad = (
        lax.psum_scatter(
            fc1_whole.astype(jnp.bfloat16), "tp", scatter_dimension=1, tiled=True
        ).astype(jnp.float32),
        lax.psum_scatter(
            fc2_whole.astype(jnp.bfloat16), "tp", scatter_dimension=0, tiled=True
        ).astype(jnp.float32),
    )
    normed_two_grad = contract_cols(hidden_grad, fc1_all)
    _, norm_two_pull = jax.vjp(layer_norm, middle, gain_b, shift_b)
    middle_part, gain_b_grad, shift_b_grad = norm_two_pull(normed_two_grad)
    middle_grad = out_grad + middle_part
    proj_bias_grad = jnp.sum(middle_grad, axis=0)
    middle_low = middle_grad.astype(jnp.bfloat16)
    middle_low_use = lax.all_gather(middle_low, "tp", axis=0, tiled=True)
    proj_local = contract_rows(mixed, middle_low_use)
    mixed_grad = contract_cols(middle_low_use, proj_use).astype(jnp.bfloat16)
    mixed_grad_win = to_windows(mixed_grad.reshape(-1, heads_now, HEAD_DIM), attn_images)
    scores = window_scores(query_win, key_win, offsets, masks, attn_images)
    probs = jnp.exp(scores - log_total)
    probs_grad = jnp.einsum(
        "wqhd,wkhd->whqk", mixed_grad_win, value_win, preferred_element_type=jnp.float32
    )
    value_grad = jnp.einsum(
        "whqk,wqhd->wkhd",
        probs.astype(jnp.bfloat16),
        mixed_grad_win,
        preferred_element_type=jnp.float32,
    ).astype(jnp.bfloat16)
    weighted = jnp.sum(probs * probs_grad, axis=-1, keepdims=True)
    score_grad = (probs * (probs_grad - weighted)).astype(jnp.bfloat16)
    summed_scores = jnp.sum(score_grad, axis=0, dtype=jnp.float32).reshape(
        heads_now, WIN * WIN * WIN * WIN
    )
    table_grad = place_part(jnp.dot(summed_scores, onehot, precision=HIGHEST), HEADS, head_start)
    query_grad = (
        jnp.einsum("whqk,wkhd->wqhd", score_grad, key_win, preferred_element_type=jnp.float32)
        * scale
    ).astype(jnp.bfloat16)
    key_grad = (
        jnp.einsum("whqk,wqhd->wkhd", score_grad, query_win, preferred_element_type=jnp.float32)
        * scale
    ).astype(jnp.bfloat16)
    query_tok = from_windows(query_grad, attn_images)
    key_tok = from_windows(key_grad, attn_images)
    value_tok = from_windows(value_grad, attn_images)
    project_grad = jnp.stack((query_tok, key_tok, value_tok), axis=2).reshape(
        -1, heads_now * 3 * HEAD_DIM
    )
    qv_sums = jnp.stack(
        (
            jnp.sum(query_tok, axis=0, dtype=jnp.float32),
            jnp.sum(value_tok, axis=0, dtype=jnp.float32),
        ),
        axis=1,
    )
    qv_bias_grad = place_part(qv_sums.reshape(-1), 2 * D, head_start * 2 * HEAD_DIM)
    qkv_local = contract_rows(normed_use, project_grad)
    qkv_wgrad, proj_wgrad = (qkv_local, proj_local)
    normed_grad = lax.psum_scatter(
        contract_cols(project_grad, qkv_use).astype(jnp.bfloat16),
        "tp",
        scatter_dimension=0,
        tiled=True,
    ).astype(jnp.float32)
    _, norm_one_pull = jax.vjp(layer_norm, layer_in, gain_a, shift_a)
    input_part, gain_a_grad, shift_a_grad = norm_one_pull(normed_grad)
    in_grad = middle_grad + input_part
    grad_w_qkv, grad_w_proj, grad_w_fc1, grad_w_fc2 = (
        lax.psum_scatter(qkv_wgrad, "dp", scatter_dimension=0, tiled=True),
        lax.psum_scatter(proj_wgrad, "dp", scatter_dimension=1, tiled=True),
        lax.psum_scatter(fc1_wgrad, "dp", scatter_dimension=0, tiled=True),
        lax.psum_scatter(fc2_wgrad, "dp", scatter_dimension=1, tiled=True),
    )
    summed = lax.psum(
        (
            qv_bias_grad,
            proj_bias_grad,
            fc1_bias_grad,
            fc2_bias_grad,
            gain_a_grad,
            shift_a_grad,
            gain_b_grad,
            shift_b_grad,
            table_grad,
        ),
        ("dp", "tp"),
    )
    shards = [
        lax.dynamic_slice_in_dim(
            vector, dp_here * (vector.shape[0] // dp_size), vector.shape[0] // dp_size
        )
        for vector in summed[:8]
    ]
    return (
        layer_out,
        in_grad,
        grad_w_qkv,
        shards[0],
        grad_w_proj,
        shards[1],
        grad_w_fc1,
        shards[2],
        grad_w_fc2,
        shards[3],
        shards[4],
        shards[5],
        shards[6],
        shards[7],
        summed[8],
    )


def solution(mesh):
    in_specs = (
        P(("dp", "tp"), None),
        P(("dp", "tp"), None),
        P("dp", "tp"),
        P("dp"),
        P("tp", "dp"),
        P("dp"),
        P("dp", "tp"),
        P("dp"),
        P("tp", "dp"),
        P("dp"),
        P("dp"),
        P("dp"),
        P("dp"),
        P("dp"),
        P(),
        P(),
    )
    out_specs = (
        P(("dp", "tp"), None),
        P(("dp", "tp"), None),
        P("dp", "tp"),
        P("dp"),
        P("tp", "dp"),
        P("dp"),
        P("dp", "tp"),
        P("dp"),
        P("tp", "dp"),
        P("dp"),
        P("dp"),
        P("dp"),
        P("dp"),
        P("dp"),
        P(),
    )
    return jax.shard_map(
        per_device, mesh=mesh, in_specs=in_specs, out_specs=out_specs, check_vma=False
    )
```

profile of v0, /device:TPU:0, one launch (start us, length us, event | category | flops | bytes accessed | tf_op | source)
XLA Modules:
  0.0 1283.4 jit_solution(2343487623124965510)
XLA Ops:
  15.7 36.0 %all-reduce.8 = (bf16[1024]{0:T(1024)(128)(2,1)S(1)}, bf16[512]{0:T(512)(128)(2,1)S(1)}, bf16[512]{0:T(512)(128)(2,1)S(1)}, bf16[512]{0:T(512)(128)(2,1)}, bf16[...) all-reduce(bf16[1024]{0:T(1024)(128)(2,1)S(1)} %dynamic-update-slic, ...), channel_id=1, replica_groups=mesh['dp'=16,'tp'=2] {'dp'}, use_global_device_ids=true, to_apply=%add.2 | all-reduce | flops 4096 | bytes 16384
  63.1 19.6 %all_gather.53 = bf16[512,768]{1,0:T(8,128)(2,1)S(1)} all-gather(bf16[32,768]{1,0:T(8,128)(2,1)S(1)} %copy-done.32), channel_id=1, replica_groups=mesh['dp'=16,'tp'=2] {'dp'}, dimensions={0}, use_global_device_ids=true | all-gather | bytes 835584 | tf_op jit(solution)/shard_map/all_gather | solution.py:119
  84.8 21.6 %all_gather.55 = bf16[256,512]{0,1:T(8,128)(2,1)} all-gather(bf16[256,32]{0,1:T(8,128)(2,1)S(1)} %copy-done.34), channel_id=1, replica_groups=mesh['dp'=16,'tp'=2] {'dp'}, dimensions={1}, use_global_device_ids=true | all-gather | bytes 278528 | tf_op jit(solution)/shard_map/all_gather | solution.py:120
  106.5 16.2 %all-gather.8.cloned.1.call-done = bf16[4704,512]{1,0:T(8,128)(2,1)} async-done(((bf16[2352,512]{1,0:T(8,128)(2,1)}), bf16[4704,512]{1,0:T(8,128)(2,1)}) %all-gather.8.cloned.1.call-update) | async-done | bytes 4816912 | tf_op jit(solution)/shard_map/all_gather | solution.py:141
  137.6 12.5 copy.106
  185.7 12.3 copy.104
  198.0 11.9 add_convert_fusion.2
  237.4 12.3 copy.110
  270.8 12.1 copy.111
  284.7 16.5 %fusion.49 = (f32[96,8,49]{2,1,0:T(8,128)}, f32[96,8,49,49]{2,3,1,0:T(8,128)}) fusion(f32[96,49,49]{1,2,0:T(8,128)} %bitcast.132, f32[8,49,49]{1,2,0:T(8,128)} %copy.112, bf16[96,49,8,32]{1,3,2,0:T(8,128)(2,1)} %copy.110, bf16[96,49,8,32]{1,3,2,0:T(8,128)(2,1)} %copy.111), kind=kOutput, calls=%fused_computation.129 | convolution fusion | flops 125352192 | bytes 13342112 | tf_op jit(solution)/shard_map/wqhd,wkhd->whqk/dot_general | solution.py:56
  333.2 12.2 copy.113
  345.4 13.8 %convolution_bitcast_fusion = bf16[96,49,8,32]{1,3,2,0:T(8,128)(2,1)} fusion(bf16[96,49,8,32]{1,3,2,0:T(8,128)(2,1)} %copy.113, f32[96,8,49,49]{2,3,1,0:T(8,128)} %get-tuple-element.118, f32[96,8,49]{2,1,0:T(8,128)S(1)} %copy-done.11), kind=kOutput, calls=%fused_computation.90 | convolution fusion | flops 121701888 | bytes 12343296 | tf_op jit(solution)/shard_map/whqk,wkhd->wqhd/dot_general | solution.py:163
  359.2 12.2 copy.115
  420.6 21.8 %all-gather = bf16[16,1,128]{2,1,0:T(2,128)(2,1)S(1)} all-gather(bf16[1,1,128]{2,1,0:T(2,128)(2,1)S(1)} %bitcast.146), channel_id=1, replica_groups=mesh['dp'=16,'tp'=2] {'dp'}, dimensions={0}, use_global_device_ids=true | all-gather | bytes 4352 | tf_op jit(solution)/shard_map/all_gather | solution.py:125
  442.6 38.7 %reduce-scatter.11.cloned.1.call-done = bf16[2352,512]{1,0:T(8,128)(2,1)} async-done(((bf16[4704,512]{1,0:T(8,128)(2,1)}), bf16[2352,512]{1,0:T(8,128)(2,1)}) %reduce-scatter.11.cloned.1.call-update) | async-done | bytes 2408464 | tf_op jit(solution)/shard_map/reduce_scatter | solution.py:169
  488.9 27.0 %all-gather.12.cloned.1.call-done = bf16[512,2048]{1,0:T(8,128)(2,1)} async-done(((bf16[512,1024]{1,0:T(8,128)(2,1)}), bf16[512,2048]{1,0:T(8,128)(2,1)}) %all-gather.12.cloned.1.call-update) | async-done | bytes 2097168 | tf_op jit(solution)/shard_map/all_gather | solution.py:178
  515.9 50.4 %multiply_convert_fusion.1 = (bf16[2352,2048]{1,0:T(8,128)(2,1)}, f32[2352,2048]{1,0:T(8,128)}, f32[2352,2048]{1,0:T(8,128)}) fusion(f32[2048]{0:T(1024)S(1)} %bitcast.144, bf16[512,2048]{1,0:T(8,128)(2,1)} %all-gather.12.cloned.1.call-done, f32[2352,512]{1,0:T(8,128)} %copy-done.3, f32[512]{0:T(512)S(1)} %convert_element_type.164, ...), kind=kOutput, calls=%fused_computation.12 | convolution fusion | flops 5256437760 | bytes 55114112 | tf_op jit(solution)/shard_map/dot_general | solution.py:181
  566.3 25.0 %convert_reduce_fusion.1 = (f32[2048]{0:T(1024)}, bf16[2352,2048]{1,0:T(8,128)(2,1)}) fusion(f32[2352,2048]{1,0:T(8,128)} %get-tuple-element.109, bf16[2048,512]{0,1:T(8,128)(2,1)} %all-gather.16.cloned.1.call-done, f32[2352,512]{1,0:T(8,128)} %param.17, f32[2352,2048]{1,0:T(8,128)} %get-tuple-element.119, f32[2048]{0:T(1024)S(1)} %bitcast.145), kind=kOutput, calls=%fused_computation.8 | convolution fusion | flops 5015590912 | bytes 55099392 | tf_op jit(solution)/shard_map/dot_general | solution.py:74
  610.9 12.4 convolution_convert_fusion.4
  634.7 40.0 %all-gather.18.cloned.1.call-done = bf16[4704,512]{1,0:T(8,128)(2,1)} async-done(((bf16[2352,512]{1,0:T(8,128)(2,1)}), bf16[4704,512]{1,0:T(8,128)(2,1)}) %all-gather.18.cloned.1.call-update) | async-done | bytes 4816912 | tf_op jit(solution)/shard_map/all_gather | solution.py:212
  708.5 12.5 copy.118
  721.0 22.2 %multiply_reduce_fusion = (f32[96,8,49]{2,1,0:T(8,128)S(1)}, f32[96,8,49,49]{2,3,1,0:T(8,128)}) fusion(f32[96,8,49,49]{2,3,1,0:T(8,128)} %get-tuple-element.118, f32[96,8,49]{2,1,0:T(8,128)S(1)} %copy-done.12, bf16[96,49,8,32]{1,3,2,0:T(8,128)(2,1)} %copy.118, bf16[96,49,8,32]{1,3,2,0:T(8,128)(2,1)} %copy.113), kind=kOutput, calls=%fused_computation.3 | convolution fusion | flops 123508224 | bytes 19869696 | tf_op jit(solution)/shard_map/wqhd,wkhd->whqk/dot_general | solution.py:218
  743.1 19.5 %convert_reduce_fusion = (f32[8,49,49]{1,2,0:T(8,128)S(1)}, bf16[96,8,49,49]{2,3,1,0:T(8,128)(2,1)}) fusion(f32[96,8,49,49]{2,3,1,0:T(8,128)} %get-tuple-element.122, f32[96,8,49]{2,1,0:T(8,128)S(1)} %get-tuple-element.121, f32[96,8,49,49]{2,3,1,0:T(8,128)} %get-tuple-element.118, f32[96,8,49]{2,1,0:T(8,128)S(1)} %copy-done.12), kind=kLoop, calls=%fused_computation.1 | loop fusion | flops 11044600 | bytes 18817568 | tf_op jit(solution)/shard_map/reduce_sum | solution.py:229
  770.6 12.4 copy.122
  801.3 13.9 %convert_bitcast_fusion = bf16[96,49,8,32]{1,3,2,0:T(8,128)(2,1)} fusion(bf16[96,49,8,32]{1,3,2,0:T(8,128)(2,1)} %copy.118, f32[96,8,49,49]{2,3,1,0:T(8,128)} %get-tuple-element.118, f32[96,8,49]{2,1,0:T(8,128)S(1)} %copy-done.12), kind=kOutput, calls=%fused_computation.74 | convolution fusion | flops 122906112 | bytes 12343296 | tf_op jit(solution)/shard_map/whqk,wqhd->wkhd/dot_general | solution.py:221
  815.1 12.2 copy.130
  857.5 12.2 copy.126
  997.5 25.9 %reduce-scatter.13.cloned.1.call-done = bf16[2352,512]{1,0:T(8,128)(2,1)} async-done(((bf16[4704,512]{1,0:T(8,128)(2,1)}), bf16[2352,512]{1,0:T(8,128)(2,1)}) %reduce-scatter.13.cloned.1.call-update) | async-done | bytes 2408464 | tf_op jit(solution)/shard_map/reduce_scatter | solution.py:257
  1033.6 40.0 %all-reduce.7 = (f32[1024]{0:T(1024)S(1)}, f32[512]{0:T(512)S(1)}, f32[2048]{0:T(1024)S(1)}, f32[512]{0:T(512)S(1)}, f32[512]{0:T(512)S(1)}, /*index=5*/f32[512]...) all-reduce(f32[1024]{0:T(1024)S(1)} %dynamic_update_slice.6, ...), channel_id=1, replica_groups=mesh['dp'=16,'tp'=2] {'dp','tp'}, use_global_device_ids=true, to_apply=%region_16.17 | all-reduce | flops 8848 | bytes 70784 | tf_op jit(solution)/shard_map/psum | solution.py:272
  1086.1 60.5 %reduce-scatter.15.cloned.1.call-done = f32[32,768]{1,0:T(8,128)} async-done(((f32[512,768]{1,0:T(8,128)}), f32[32,768]{1,0:T(8,128)}) %reduce-scatter.15.cloned.1.call-update) | async-done | bytes 98320 | tf_op jit(solution)/shard_map/reduce_scatter | solution.py:267
  1146.6 64.9 %reduce-scatter.21.cloned.1.call-done = f32[32,1024]{1,0:T(8,128)} async-done(((f32[512,1024]{1,0:T(8,128)}), f32[32,1024]{1,0:T(8,128)}) %reduce-scatter.21.cloned.1.call-update) | async-done | bytes 131088 | tf_op jit(solution)/shard_map/reduce_scatter | solution.py:269
  1211.5 65.2 %reduce-scatter.25.cloned.1.call-done = f32[32,1024]{1,0:T(8,128)} async-done(((f32[512,1024]{1,0:T(8,128)}), f32[32,1024]{1,0:T(8,128)}) %reduce-scatter.25.cloned.1.call-update) | async-done | bytes 131088
  (299 shorter events, 481.3 us)
Async XLA Ops:
  7.2 75.8 %copy-start = (bf16[16,169]{1,0:T(8,128)(2,1)S(1)}, bf16[16,169]{1,0:T(8,128)(2,1)}, u32[]{:S(2)}) copy-start(bf16[16,169]{1,0:T(8,128)(2,1)} %param.30) | copy-start | bytes 16228
  7.2 115.5 %all-gather.8.cloned.1.call-start = ((), (), s32[]{:S(2)}) async-start(), calls=%async_computation.8 | async-start | bytes 7225344 | tf_op jit(solution)/shard_map/all_gather | solution.py:141
  54.5 30.3 %copy-start.34 = (bf16[256,32]{0,1:T(8,128)(2,1)S(1)}, bf16[256,32]{0,1:T(8,128)(2,1)}, u32[]{:S(2)}) copy-start(bf16[256,32]{0,1:T(8,128)(2,1)} %param.20) | copy-start | bytes 49156
  61.5 358.5 %all-gather.10.cloned.1.call-start = ((), (), s32[]{:S(2)}) async-start(), calls=%async_computation.10 | async-start | bytes 1114112 | tf_op jit(solution)/shard_map/all_gather | solution.py:121
  62.3 380.2 %all-gather.14.cloned.1.call-start = ((), (), s32[]{:S(2)}) async-start(), calls=%async_computation.12 | async-start | bytes 1114112 | tf_op jit(solution)/shard_map/all_gather | solution.py:122
  63.0 418.2 %reduce-scatter.11.cloned.1.call-start = ((), (), s32[]{:S(2)}) async-start(), calls=%async_computation.9 | async-start | bytes 7225344 | tf_op jit(solution)/shard_map/reduce_scatter | solution.py:169
  82.7 46.8 %copy-start.20 = (bf16[512,768]{1,0:T(8,128)(2,1)}, bf16[512,768]{1,0:T(8,128)(2,1)S(1)}, u32[]{:S(2)}) copy-start(bf16[512,768]{1,0:T(8,128)(2,1)S(1)} %all_gather.53) | copy-start | bytes 2359300
  185.7 34.8 %slice-start.8 = ((s8[7569408]{0:T(1024)(128)(4,1)}), s8[3375104]{0:T(1024)(128)(4,1)S(1)}, s32[]{:S(2)}) async-start(s8[7569408]{0:T(1024)(128)(4,1)} %bitcast.103), calls=%async_computation.30 | async-start | bytes 6750208
  284.7 33.1 %slice-start.4 = ((s8[7569408]{0:T(1024)(128)(4,1)}), s8[3375104]{0:T(1024)(128)(4,1)S(1)}, s32[]{:S(2)}) async-start(s8[7569408]{0:T(1024)(128)(4,1)} %bitcast.99), calls=%async_computation.26 | async-start | bytes 6750208
  419.9 95.9 %all-gather.12.cloned.1.call-start = ((), (), s32[]{:S(2)}) async-start(), calls=%async_computation.11 | async-start | bytes 3145728 | tf_op jit(solution)/shard_map/all_gather | solution.py:178
  420.5 145.7 %all-gather.16.cloned.1.call-start = ((), (), s32[]{:S(2)}) async-start(), calls=%async_computation.13 | async-start | bytes 3145728 | tf_op jit(solution)/shard_map/all_gather | solution.py:179
  442.5 232.2 %all-gather.18.cloned.1.call-start = ((), (), s32[]{:S(2)}) async-start(), calls=%async_computation.14 | async-start | bytes 7225344 | tf_op jit(solution)/shard_map/all_gather | solution.py:212
  610.8 367.4 %reduce-scatter.19.cloned.1.call-start = ((), (), s32[]{:S(2)}) async-start(), calls=%async_computation.18 | async-start | bytes 3145728 | tf_op jit(solution)/shard_map/reduce_scatter | solution.py:199
  623.3 358.1 %reduce-scatter.23.cloned.1.call-start = ((), (), s32[]{:S(2)}) async-start(), calls=%async_computation.20 | async-start | bytes 3145728 | tf_op jit(solution)/shard_map/reduce_scatter | solution.py:202
  623.3 51.4 %copy-start.19 = (bf16[256,512]{0,1:T(8,128)(2,1)S(1)}, bf16[256,512]{0,1:T(8,128)(2,1)}, u32[]{:S(2)}) copy-start(bf16[256,512]{0,1:T(8,128)(2,1)} %all_gather.55) | copy-start | bytes 786436
  634.7 388.8 %reduce-scatter.13.cloned.1.call-start = ((), (), s32[]{:S(2)}) async-start(), calls=%async_computation.15 | async-start | bytes 7225344 | tf_op jit(solution)/shard_map/reduce_scatter | solution.py:257
  708.5 54.1 %slice-start.2 = ((s8[6291456]{0:T(1024)(128)(4,1)}), s8[2097152]{0:T(1024)(128)(4,1)S(1)}, s32[]{:S(2)}) async-start(s8[6291456]{0:T(1024)(128)(4,1)} %bitcast.95), calls=%async_computation.24 | async-start | bytes 4194304
  721.0 41.7 %slice-start.3 = ((s8[6291456]{0:T(1024)(128)(4,1)}), s8[4194304]{0:T(1024)(128)(4,1)S(1)}, s32[]{:S(2)}) async-start(s8[6291456]{0:T(1024)(128)(4,1)} %bitcast.95), calls=%async_computation.25 | async-start | bytes 8388608
  962.4 123.8 %reduce-scatter.17.cloned.1.call-start = ((), (), s32[]{:S(2)}) async-start(), calls=%async_computation.17 | async-start | bytes 557056 | tf_op jit(solution)/shard_map/reduce_scatter | solution.py:268
  967.7 178.9 %reduce-scatter.15.cloned.1.call-start = ((), (), s32[]{:S(2)}) async-start(), calls=%async_computation.16 | async-start | bytes 1671168 | tf_op jit(solution)/shard_map/reduce_scatter | solution.py:267
  978.2 233.3 %reduce-scatter.21.cloned.1.call-start = ((), (), s32[]{:S(2)}) async-start(), calls=%async_computation.19 | async-start | bytes 2228224 | tf_op jit(solution)/shard_map/reduce_scatter | solution.py:269
  981.3 295.4 %reduce-scatter.25.cloned.1.call-start = ((), (), s32[]{:S(2)}) async-start(), calls=%async_computation.21 | async-start | bytes 2228224
  984.2 39.3 %copy-start.23 = (f32[2352]{0:T(1024)S(1)}, f32[2352]{0:T(1024)}, u32[]{:S(2)}) copy-start(f32[2352]{0:T(1024)} %copy-done.22) | copy-start | bytes 28228
  984.2 39.3 %copy-start.31 = (f32[512]{0:T(512)S(1)}, f32[512]{0:T(512)}, u32[]{:S(2)}) copy-start(f32[512]{0:T(512)} %copy-done.30) | copy-start | bytes 6148
  995.9 32.9 %copy-start.27 = (f32[2352]{0:T(1024)S(1)}, f32[2352]{0:T(1024)}, u32[]{:S(2)}) copy-start(f32[2352]{0:T(1024)} %copy-done.26) | copy-start | bytes 28228
  995.9 32.9 %copy-start.25 = (f32[2352]{0:T(1024)S(1)}, f32[2352]{0:T(1024)}, u32[]{:S(2)}) copy-start(f32[2352]{0:T(1024)} %copy-done.24) | copy-start | bytes 28228
  996.6 37.0 %copy-start.37 = (f32[512]{0:T(512)S(1)}, f32[512]{0:T(512)}, u32[]{:S(2)}) copy-start(f32[512]{0:T(512)} %get-tuple-element.100) | copy-start | bytes 6148
  996.6 37.0 %copy-start.38 = (f32[512]{0:T(512)S(1)}, f32[512]{0:T(512)}, u32[]{:S(2)}) copy-start(f32[512]{0:T(512)} %get-tuple-element.114) | copy-start | bytes 6148
  996.6 37.0 %copy-start.39 = (f32[2048]{0:T(1024)S(1)}, f32[2048]{0:T(1024)}, u32[]{:S(2)}) copy-start(f32[2048]{0:T(1024)} %get-tuple-element.123) | copy-start | bytes 24580
  996.6 37.0 %copy-start.40 = (f32[512]{0:T(512)S(1)}, f32[512]{0:T(512)}, u32[]{:S(2)}) copy-start(f32[512]{0:T(512)} %get-tuple-element.75) | copy-start | bytes 6148
  996.6 37.0 %copy-start.41 = (f32[512]{0:T(512)S(1)}, f32[512]{0:T(512)}, u32[]{:S(2)}) copy-start(f32[512]{0:T(512)} %get-tuple-element.79) | copy-start | bytes 6148
  1078.3 198.4 %copy-start.1 = (bf16[16,169]{1,0:T(8,128)(2,1)S(1)}, bf16[16,169]{1,0:T(8,128)(2,1)}, u32[]{:S(2)}) copy-start(bf16[16,169]{1,0:T(8,128)(2,1)} %param.30) | copy-start | bytes 16228
  (45 other events, 416.0 us)
Sparse Core Ops, SparseCore 0:
  61.7 61.0 all-gather.7
  124.9 37.9 all-gather.9
  165.0 36.8 all-gather.13
  420.0 61.1 reduce-scatter.10
  482.7 33.1 all-gather.11
  517.3 33.1 all-gather.15
  610.9 63.7 all-gather.17
  677.1 31.8 reduce-scatter.18
  711.2 31.8 reduce-scatter.22
  962.5 60.9 reduce-scatter.12
  1027.6 55.8 reduce-scatter.16
  1088.0 58.5 reduce-scatter.14
  1150.9 60.5 reduce-scatter.20
  1216.1 60.4 reduce-scatter.24
where the time goes:
time: 1300 us; the launch traced here: 1280 us
  local copies, waits for them, and re-layouts  364 us (28%)
  waiting for transfers between devices  341 us (26%)
  matrix products  245 us (19%)
  other arithmetic  178 us (14%)
  blocking collectives  139 us (11%)
  between operations  16.3 us (1%)
    unnamed x15, waiting for transfers between devices  67.2 us
    reduce_scatter x1, waiting for transfers between devices, per_device(): lax.psum_scatter(fc1_wgrad, 'dp', scatter_dimension=0, tiled=True)  64.9 us
    reduce_scatter x1, waiting for transfers between devices, per_device(): lax.psum_scatter(qkv_wgrad, 'dp', scatter_dimension=0, tiled=True)  60.5 us
    dot_general x1, matrix products, per_device(): jnp.dot(normed_two, fc1_all, preferred_element_type=jnp.float32) + bias_fc1  50.4 us
    reshape x4, local copies, waits for them, and re-layouts, to_windows(): return lattice.reshape((images * per_side * per_side, WIN * WIN) + inner)  49 us
    dot_general x4, matrix products, contract_cols(): lax.dot_general(left, right, (((1,), (1,)), ((), ())), preferred_element_...  46.5 us
    all_gather x1, waiting for transfers between devices, per_device(): middle_low_use = lax.all_gather(middle_low, 'tp', axis=0, tiled=True)  40 us
    psum x1, blocking collectives, per_device(): lax.psum((qv_bias_grad, proj_bias_grad, fc1_bias_grad, fc2_bias_grad, gai...  40 us
  transfers between devices with their start and end apart: 14, of which 8 were waited for; matrix products, arithmetic and copies ran while one was open for 56% of the time, Pallas kernels for 0%

commit v1 on v0

v1 whole, which is shorter than its diff:
```python
import functools

import jax
import jax.numpy as jnp
from jax import lax
from jax.experimental import pallas as pl
from jax.experimental.pallas import tpu as pltpu
from jax.sharding import PartitionSpec as P

D = 512
HEADS = 16
HEAD_DIM = 32
FF = 2048
RES = 14
WIN = 7
SHIFT = 3
TBL = 169
PLACES = WIN * WIN
PAD = 64
PAIR = 2
ROWS = PAIR * RES * RES
WROWS = PAIR * 4 * PAD
GROUPS = 4
LANES = 128
SCALE = HEAD_DIM ** (-0.5)
QKV, PROJ, FC1, FC2 = 0, 768, 1024, 2048
COLS = 3072
CHUNK = 512
EPS = 1e-05
HIGHEST = lax.Precision.HIGHEST


def dot(left, right, dims=(1, 0)):
    return lax.dot_general(
        left, right, (((dims[0],), (dims[1],)), ((), ())), preferred_element_type=jnp.float32
    )


def row_sum(value):
    return jnp.sum(value, axis=0, keepdims=True)


def norm_parts(value):
    centred = value - jnp.mean(value, axis=-1, keepdims=True)
    inverse = lax.rsqrt(jnp.mean(centred * centred, axis=-1, keepdims=True) + EPS)
    return centred * inverse, inverse


def norm_back(upstream, hat, inverse, gain):
    scaled = upstream * gain
    return (
        scaled
        - jnp.mean(scaled, axis=-1, keepdims=True)
        - hat * jnp.mean(scaled * hat, axis=-1, keepdims=True)
    ) * inverse


def pick_heads(stacked):
    lane = lax.broadcasted_iota(jnp.int32, (PAD, LANES), 1)
    parts = [stacked[h * PAD : (h + 1) * PAD] for h in range(4)]
    low = jnp.where(lane < 32, parts[0], parts[1])
    high = jnp.where(lane < 96, parts[2], parts[3])
    return jnp.where(lane < 64, low, high)


def block_kernel(
    x_ref, og_ref, w_ref, vec_ref, b1_ref, bias_ref, to_win_ref, to_tok_ref, hm_ref,
    out_ref, ig_ref, gw_ref, gvec_ref, gb1_ref, gtab_ref,
    acc_ref, qkv_ref, mixw_ref, probs_ref, pg_ref, dmw_ref, nw_ref, mo_ref, dn_ref,
):
    bf16, f32 = jnp.bfloat16, jnp.float32
    step = pl.program_id(0)

    @pl.when(step == 0)
    def _():
        acc_ref[...] = jnp.zeros_like(acc_ref)
        gvec_ref[...] = jnp.zeros_like(gvec_ref)
        gb1_ref[...] = jnp.zeros_like(gb1_ref)
        gtab_ref[...] = jnp.zeros_like(gtab_ref)

    def vec(row):
        return vec_ref[row : row + 1, :]

    hat, _ = norm_parts(x_ref[...])
    normed = (hat * vec(4) + vec(5)).astype(bf16)
    nw_ref[...] = dot(to_win_ref[...], normed).astype(bf16)
    for t in range(2):
        half = slice(t * 256, t * 256 + 256)
        project = dot(nw_ref[...], w_ref[t, :, QKV:PROJ])
        qkv_ref[t, :, 0:256] = (project[:, 0:256] + vec_ref[0:1, half]).astype(bf16)
        qkv_ref[t, :, 256:512] = project[:, 256:512].astype(bf16)
        qkv_ref[t, :, 512:768] = (project[:, 512:768] + vec_ref[1:2, half]).astype(bf16)

    def spread(value):
        return jnp.concatenate([value] * 4, axis=0) * hm_ref[...]

    @pl.loop(0, PAIR * 4)
    def _(w):
        rows = pl.ds(pl.multiple_of(w * PAD, PAD), PAD)
        place = lax.rem(w, 4)
        for g in range(GROUPS):
            t, base = g // 2, (g % 2) * LANES
            q = spread(qkv_ref[t, rows, base : base + LANES])
            k = qkv_ref[t, rows, 256 + base : 256 + base + LANES]
            v = qkv_ref[t, rows, 512 + base : 512 + base + LANES]
            scores = dot(q, k, (1, 1)) * SCALE + bias_ref[place, g]
            powers = jnp.exp(scores - jnp.max(scores, axis=-1, keepdims=True))
            probs = powers * (1.0 / jnp.sum(powers, axis=-1, keepdims=True))
            probs_ref[w, g] = probs
            mixed = pick_heads(dot(probs.astype(bf16), v))
            mixw_ref[rows, g * LANES : (g + 1) * LANES] = mixed.astype(bf16)

    mix = dot(to_tok_ref[...], mixw_ref[...]).astype(bf16)
    attn = dot(mix[:, 0:256], w_ref[0, :, PROJ:FC1], (1, 1)) + dot(
        mix[:, 256:512], w_ref[1, :, PROJ:FC1], (1, 1)
    )
    middle = x_ref[...] + attn + vec(2)
    hat2, inverse2 = norm_parts(middle)
    normed_two = (hat2 * vec(6) + vec(7)).astype(bf16)
    out_low = og_ref[...].astype(bf16)
    mo_ref[...] = middle + vec(3)
    dn_ref[...] = jnp.zeros_like(dn_ref)

    @pl.loop(0, 2)
    def _(t):
        for j in range(1024 // CHUNK):
            one = slice(FC1 + j * CHUNK, FC1 + (j + 1) * CHUNK)
            two = slice(FC2 + j * CHUNK, FC2 + (j + 1) * CHUNK)
            cols = slice(j * CHUNK, (j + 1) * CHUNK)
            hidden = dot(normed_two, w_ref[t, :, one]) + b1_ref[t, :, cols]
            cdf = 0.5 + 0.5 * lax.erf(hidden * (0.5**0.5))
            active = (hidden * cdf).astype(bf16)
            mo_ref[...] += dot(active, w_ref[t, :, two], (1, 1))
            slope = cdf + hidden * (jnp.exp(hidden * hidden * -0.5) * 0.3989422804014327)
            hidden_grad = (dot(out_low, w_ref[t, :, two]) * slope).astype(bf16)
            dn_ref[...] += dot(hidden_grad, w_ref[t, :, one], (1, 1))
            acc_ref[t, :, two] += dot(out_low, active, (0, 0))
            acc_ref[t, :, one] += dot(normed_two, hidden_grad, (0, 0))
            gb1_ref[t, :, cols] += row_sum(hidden_grad.astype(f32))

    out_ref[...] = mo_ref[...]
    upstream = dn_ref[...]
    out_grad = og_ref[...]
    middle_grad = out_grad + norm_back(upstream, hat2, inverse2, vec(6))
    mo_ref[...] = middle_grad
    gvec_ref[2:3, :] += row_sum(middle_grad)
    gvec_ref[3:4, :] += row_sum(out_grad)
    gvec_ref[6:7, :] += row_sum(upstream * hat2)
    gvec_ref[7:8, :] += row_sum(upstream)
    middle_low = middle_grad.astype(bf16)
    middle_win = dot(to_win_ref[...], middle_low).astype(bf16)
    for t in range(2):
        half = slice(t * 256, t * 256 + 256)
        dmw_ref[:, half] = dot(middle_win, w_ref[t, :, PROJ:FC1]).astype(bf16)
        acc_ref[t, :, PROJ:FC1] += dot(middle_low, mix[:, half], (0, 0))

    @pl.loop(0, PAIR * 4)
    def _(w):
        rows = pl.ds(pl.multiple_of(w * PAD, PAD), PAD)
        for g in range(GROUPS):
            t, base = g // 2, (g % 2) * LANES
            q = spread(qkv_ref[t, rows, base : base + LANES])
            k = qkv_ref[t, rows, 256 + base : 256 + base + LANES]
            v = qkv_ref[t, rows, 512 + base : 512 + base + LANES]
            up = spread(dmw_ref[rows, g * LANES : (g + 1) * LANES])
            probs = probs_ref[w, g]
            probs_grad = dot(up, v, (1, 1))
            weighted = jnp.sum(probs * probs_grad, axis=-1, keepdims=True)
            score_grad = (probs * (probs_grad - weighted)).astype(bf16)
            gtab_ref[g] += score_grad.astype(f32)
            dq = pick_heads(dot(score_grad, k)) * SCALE
            dk = dot(score_grad, q, (0, 0)) * SCALE
            dv = dot(probs.astype(bf16), up, (0, 0))
            pg_ref[t, rows, base : base + LANES] = dq.astype(bf16)
            pg_ref[t, rows, 256 + base : 256 + base + LANES] = dk.astype(bf16)
            pg_ref[t, rows, 512 + base : 512 + base + LANES] = dv.astype(bf16)

    for t in range(2):
        half = slice(t * 256, t * 256 + 256)
        acc_ref[t, :, QKV:PROJ] += dot(nw_ref[...], pg_ref[t], (0, 0))
        gvec_ref[0:1, half] += row_sum(pg_ref[t, :, 0:256].astype(f32))
        gvec_ref[1:2, half] += row_sum(pg_ref[t, :, 512:768].astype(f32))
    back = dot(pg_ref[0], w_ref[0, :, QKV:PROJ], (1, 1)) + dot(
        pg_ref[1], w_ref[1, :, QKV:PROJ], (1, 1)
    )
    upstream = dot(to_tok_ref[...], back.astype(bf16))
    hat, inverse = norm_parts(x_ref[...])
    gvec_ref[4:5, :] += row_sum(upstream * hat)
    gvec_ref[5:6, :] += row_sum(upstream)
    ig_ref[...] = mo_ref[...] + norm_back(upstream, hat, inverse, vec(4))

    @pl.when(step == pl.num_programs(0) - 1)
    def _():
        gw_ref[...] = acc_ref[...].astype(bf16)


def run_block(layer_in, out_grad, weights, vecs, bias_one, bias, to_win, to_tok, head_mask):
    rows = layer_in.shape[0]
    bf16, f32 = jnp.bfloat16, jnp.float32

    def whole(shape):
        return pl.BlockSpec(shape, lambda i: (0,) * len(shape), pipeline_mode=pl.Buffered(1))

    tokens = pl.BlockSpec((ROWS, D), lambda i: (i, 0))
    fixed = (weights, vecs, bias_one, bias, to_win, to_tok, head_mask)
    outs = (
        jax.ShapeDtypeStruct((rows, D), f32),
        jax.ShapeDtypeStruct((rows, D), f32),
        jax.ShapeDtypeStruct((2, D, COLS), bf16),
        jax.ShapeDtypeStruct((8, D), f32),
        jax.ShapeDtypeStruct((2, 1, FF // 2), f32),
        jax.ShapeDtypeStruct((GROUPS, 4 * PAD, PAD), f32),
    )
    return pl.pallas_call(
        block_kernel,
        grid=(rows // ROWS,),
        out_shape=outs,
        in_specs=[tokens, tokens] + [whole(member.shape) for member in fixed],
        out_specs=[tokens, tokens] + [whole(member.shape) for member in outs[2:]],
        scratch_shapes=[
            pltpu.VMEM((2, D, COLS), f32),
            pltpu.VMEM((2, WROWS, 768), bf16),
            pltpu.VMEM((WROWS, D), bf16),
            pltpu.VMEM((PAIR * 4, GROUPS, 4 * PAD, PAD), f32),
            pltpu.VMEM((2, WROWS, 768), bf16),
            pltpu.VMEM((WROWS, D), bf16),
            pltpu.VMEM((WROWS, D), bf16),
            pltpu.VMEM((ROWS, D), f32),
            pltpu.VMEM((ROWS, D), f32),
        ],
        compiler_params=pltpu.CompilerParams(
            dimension_semantics=("arbitrary",), vmem_limit_bytes=60 * 1024 * 1024
        ),
    )(layer_in, out_grad, *fixed)


def window_source():
    spot = jnp.arange(WROWS, dtype=jnp.int32)
    image, window, place = spot // (4 * PAD), (spot // PAD) % 4, spot % PAD
    row = ((window // 2) * WIN + place // WIN + SHIFT) % RES
    col = ((window % 2) * WIN + place % WIN + SHIFT) % RES
    return jnp.where(place < PLACES, image * RES * RES + row * RES + col, -1)


def score_bias(table, rel_index):
    places = jnp.arange(RES, dtype=jnp.int32)
    band_of = (places >= RES - WIN).astype(jnp.int32) + (places >= RES - SHIFT).astype(jnp.int32)
    labels = (band_of[:, None] * 3 + band_of[None, :]).reshape(2, WIN, 2, WIN)
    labels = jnp.swapaxes(labels, 1, 2).reshape(4, PLACES)
    masks = jnp.where(labels[:, :, None] != labels[:, None, :], -100.0, 0.0).astype(jnp.float32)
    gap = PAD - PLACES
    index = jnp.pad(rel_index, ((0, gap), (0, gap)), constant_values=-1).reshape(-1)
    onehot = (index[:, None] == jnp.arange(TBL, dtype=jnp.int32)[None, :]).astype(jnp.bfloat16)
    offsets = dot(table, onehot, (1, 1)).reshape(HEADS, PAD, PAD)
    masks = jnp.pad(masks, ((0, 0), (0, gap), (0, gap)))
    absent = jnp.where(jnp.arange(PAD) < PLACES, 0.0, -1e30).astype(jnp.float32)
    bias = offsets[None] + masks[:, None] + absent
    return bias.reshape(4, GROUPS, 4 * PAD, PAD), onehot


def per_device(
    layer_in, out_grad, w_qkv, b_qv, w_proj, b_proj, w_fc1, b_fc1, w_fc2, b_fc2,
    gain_one, shift_one, gain_two, shift_two, rel_table, rel_index,
):
    dp_size = lax.axis_size("dp")
    dp_here = lax.axis_index("dp")
    tp_size = lax.axis_size("tp")
    part = w_qkv.shape[0]
    both = ("dp", "tp")
    qkv_cols = w_qkv.reshape(part, 8, 3, HEAD_DIM).swapaxes(1, 2).reshape(part, 768)
    vectors = (b_qv, b_proj, b_fc2, gain_one, shift_one, gain_two, shift_two, b_fc1)
    small = jnp.concatenate(vectors).reshape(part, -1)
    small = jnp.pad(small, ((0, 0), (0, LANES - small.shape[1])))
    packed = jnp.concatenate((qkv_cols, w_proj.T, w_fc1, w_fc2.T, small), axis=1)
    spread = lax.all_gather(packed, both, axis=0, tiled=False)
    spread = spread.reshape(dp_size, tp_size, part, COLS + LANES)
    weights = spread[..., :COLS].swapaxes(0, 1).reshape(tp_size, D, COLS)
    flat = spread[:, 0, :, COLS : COLS + 12].reshape(dp_size, part * 12).astype(jnp.float32)
    pieces = []
    start = 0
    for vector in vectors:
        size = vector.shape[0]
        pieces.append(flat[:, start : start + size].reshape(-1))
        start += size
    qv = pieces[0].reshape(HEADS, 2, HEAD_DIM)
    vecs = jnp.stack((qv[:, 0].reshape(-1), qv[:, 1].reshape(-1), *pieces[1:7]))
    bias, onehot = score_bias(rel_table, rel_index)
    source = window_source()
    to_win = (source[:, None] == jnp.arange(ROWS, dtype=jnp.int32)[None, :]).astype(jnp.bfloat16)
    to_tok = (source[None, :] == jnp.arange(ROWS, dtype=jnp.int32)[:, None]).astype(jnp.bfloat16)
    head_mask = (
        jnp.arange(4 * PAD, dtype=jnp.int32)[:, None] // PAD
        == jnp.arange(LANES, dtype=jnp.int32)[None, :] // HEAD_DIM
    ).astype(jnp.bfloat16)
    layer_out, in_grad, gw, gvec, gb1, gtab = run_block(
        layer_in, out_grad, weights, vecs, pieces[7].reshape(2, 1, FF // 2), bias,
        to_win, to_tok, head_mask,
    )
    ready = gw.reshape(tp_size, dp_size, part, COLS).swapaxes(0, 1).reshape(-1, COLS)
    mine = lax.psum_scatter(ready, both, scatter_dimension=0, tiled=True).astype(jnp.float32)
    grad_qkv = mine[:, QKV:PROJ].reshape(part, 3, 8, HEAD_DIM).swapaxes(1, 2).reshape(part, 768)
    table_grad = lax.dot_general(
        gtab.reshape(HEADS, PAD * PAD),
        onehot.astype(jnp.float32),
        (((1,), (0,)), ((), ())),
        precision=HIGHEST,
        preferred_element_type=jnp.float32,
    )
    bundle = jnp.concatenate((gvec.reshape(-1), gb1.reshape(-1), table_grad.reshape(-1)))
    bundle = jnp.pad(bundle, (0, -bundle.shape[0] % 1024)).reshape(-1, LANES)
    total = jnp.sum(lax.all_gather(bundle, both, axis=0, tiled=False), axis=0).reshape(-1)
    rows = total[: 8 * D].reshape(8, D)
    qv_grad = jnp.stack(
        (rows[0].reshape(HEADS, HEAD_DIM), rows[1].reshape(HEADS, HEAD_DIM)), axis=1
    ).reshape(-1)

    def shard(vector):
        size = vector.shape[0] // dp_size
        return lax.dynamic_slice_in_dim(vector, dp_here * size, size)

    return (
        layer_out,
        in_grad,
        grad_qkv,
        shard(qv_grad),
        mine[:, PROJ:FC1].T,
        shard(rows[2]),
        mine[:, FC1:FC2],
        shard(total[8 * D : 8 * D + FF]),
        mine[:, FC2:COLS].T,
        shard(rows[3]),
        shard(rows[4]),
        shard(rows[5]),
        shard(rows[6]),
        shard(rows[7]),
        total[8 * D + FF : 8 * D + FF + HEADS * TBL].reshape(HEADS, TBL),
    )


def solution(mesh):
    tokens = P(("dp", "tp"), None)
    vector = P("dp")
    in_specs = (
        tokens, tokens, P("dp", "tp"), vector, P("tp", "dp"), vector, P("dp", "tp"), vector,
        P("tp", "dp"), vector, vector, vector, vector, vector, P(), P(),
    )
    out_specs = (
        tokens, tokens, P("dp", "tp"), vector, P("tp", "dp"), vector, P("dp", "tp"), vector,
        P("tp", "dp"), vector, vector, vector, vector, vector, P(),
    )
    return jax.shard_map(
        per_device, mesh=mesh, in_specs=in_specs, out_specs=out_specs, check_vma=False
    )
```

time: 1300 us -> 487 us (0.37); the launches traced: 1280 us -> 486 us
  local copies, waits for them, and re-layouts: 364 us -> 43.6 us
  matrix products: 245 us -> 1.95 us
  Pallas kernels: 0 us -> 192 us
  other arithmetic: 178 us -> 9.01 us
  blocking collectives: 139 us -> 0 us
  waiting for transfers between devices: 341 us -> 226 us
    dot_general x20 -> x2, matrix products: 245 us -> 1.95 us  [the longest x1 1.39 us: per_device(): lax.dot_general(gtab.reshape(HEADS, PAD * PAD), onehot.astype(jnp.float32...]
    pallas_call x0 -> x1, Pallas kernels: none -> 192 us  [run_block(): pl.pallas_call(block_kernel, grid=(rows // ROWS,), out_shape=outs, in_spe...]
    slice x22 -> x9, local copies, waits for them, and re-layouts: 111 us -> 8.27 us  [the longest x1 6.09 us: per_device(): weights = spread[..., :COLS].swapaxes(0, 1).reshape(tp_size, D, COLS)]
    reduce_scatter x7 -> x1, waiting for transfers between devices: 190 us -> 112 us  [per_device(): lax.psum_scatter(ready, both, scatter_dimension=0, tiled=True)]
    transpose x9 -> x4, local copies, waits for them, and re-layouts: 84.7 us -> 7.47 us  [the longest x1 6.16 us: per_device(): gw.reshape(tp_size, dp_size, part, COLS).swapaxes(0, 1).reshape(-1, COLS)]
    reduce_sum x12 -> x1, other arithmetic: 74 us -> 1.34 us  [per_device(): jnp.sum(lax.all_gather(bundle, both, axis=0, tiled=False), axis=0)]
    unnamed x15 -> x3, waiting for transfers between devices: 67.2 us -> 0.05 us
    all_gather x3 -> x0, blocking collectives: 63 us -> none  [the longest x1 21.8 us: per_device(): lax.all_gather(b_fc1, 'dp', axis=0, tiled=True)]
  transfers between devices with their start and end apart: 14 -> 3, of which waited for: 8 -> 3; matrix products, arithmetic and copies ran while one was open for 56% -> 4% of each run, Pallas kernels for 0% -> 0%
where the time goes in v1:
time: 487 us; the launch traced here: 486 us
  waiting for transfers between devices  226 us (46%)
  Pallas kernels  192 us (39%)
  local copies, waits for them, and re-layouts  43.6 us (9%)
  between operations  14 us (3%)
  other arithmetic  9.01 us (2%)
    pallas_call x1, Pallas kernels, run_block(): pl.pallas_call(block_kernel, grid=(rows // ROWS,), out_shape=outs, in_spe...  192 us
    reduce_scatter x1, waiting for transfers between devices, per_device(): lax.psum_scatter(ready, both, scatter_dimension=0, tiled=True)  112 us
    all_gather x1, waiting for transfers between devices, per_device(): spread = lax.all_gather(packed, both, axis=0, tiled=False)  67.1 us
    all_gather x1, waiting for transfers between devices, per_device(): lax.all_gather(bundle, both, axis=0, tiled=False)  46.6 us
    unnamed x12, local copies, waits for them, and re-layouts  9.99 us
  transfers between devices with their start and end apart: 3, of which 3 were waited for; matrix products, arithmetic and copies ran while one was open for 4% of the time, Pallas kernels for 0%

profile of v1, /device:TPU:0, one launch (start us, length us, event | category | flops | bytes accessed | tf_op | source)
XLA Modules:
  0.0 486.5 jit_solution(12815927522540852553)
XLA Ops:
  7.2 1.0 reshape.426
  8.4 5.4 %concatenate.9 = bf16[384]{0:T(512)(128)(2,1)S(1)} concatenate(bf16[64]{0:T(256)(128)(2,1)} %param.19, bf16[32]{0:T(256)(128)(2,1)} %param.21, bf16[32]{0:T(256)(128)(2,1)} %param.25, bf16[32]{0:T(256)(128)(2,1)} %param.26, bf16[32]{0:T(256)(128)(2,1)} %param.27, bf16[32]{0:T(256)(128)(2,1)} %param.28, bf16[32]{0:T(256)(128)(2,1)} %param.29, bf16[128]{0:T(256)(128)(2,1)} %param.23), dimensions={0} | concatenate | bytes 1536 | tf_op jit(solution)/shard_map/concatenate | solution.py:272
  14.0 0.7 bitcast_dynamic-update-slice_fusion.1
  14.7 0.8 constant_dynamic-update-slice_fusion.1
  15.6 0.8 bitcast_dynamic-update-slice_fusion
  16.4 0.7 copy-done.2
  17.3 0.8 pad.17
  19.2 0.7 compare_convert_fusion.hm_ref
  19.9 0.9 fusion.5.to_tok_ref
  20.7 1.0 fusion.4.to_win_ref
  21.9 1.6 fusion.1.bias_ref
  23.5 67.1 %all-gather.6.cloned.1.call-done = bf16[1024,3200]{1,0:T(8,128)(2,1)} async-done(((bf16[32,3200]{1,0:T(8,128)(2,1)}), bf16[1024,3200]{1,0:T(8,128)(2,1)}) %all-gather.6.cloned.1.call-update) | async-done | bytes 6553616 | tf_op jit(solution)/shard_map/all_gather | solution.py:275
  90.7 0.9 fusion.6
  92.5 6.1 %slice.126 = bf16[16,2,32,3072]{3,2,1,0:T(8,128)(2,1)} slice(bf16[16,2,32,3200]{3,2,1,0:T(8,128)(2,1)} %bitcast.70), slice={[0:16], [0:2], [0:32], [0:3072]} | slice | bytes 12582912 | tf_op jit(solution)/shard_map/slice | solution.py:277
  99.3 6.2 %copy.64 = bf16[16,2,32,3072]{3,2,0,1:T(8,128)(2,1)} copy(bf16[16,2,32,3072]{3,2,1,0:T(8,128)(2,1)} %slice.126) | data formatting | bytes 12582912
  105.4 0.6 stack.6.vec_ref
  106.1 192.0 %shard_map.271 = (f32[2352,512]{1,0:T(8,128)}, f32[2352,512]{1,0:T(8,128)}, bf16[2,512,3072]{2,1,0:T(8,128)(2,1)}, f32[8,512]{1,0:T(8,128)}, f32[2,1,1024]{2,1,0:T(1,128)}, /*index=5*/f32[4,256,64]{2,1,0:T(8,128)}) custom-call(f32[2352,512]{1,0:T(8,128)} %x_ref.1, f32[2352,512]{1,0:T(8,128)} %og_ref.1, bf16[2,512,3072]{2,1,0:T(8,128)(2,1)} %bitcast.67, ...), custom_call_target="tpu_custom_call" | custom-call | tf_op jit(solution)/shard_map/pallas_call | solution.py:214
  298.1 1.2 reshape.437
  299.3 1.4 fusion
  300.8 0.7 copy.68
  301.5 1.3 fusion.7
  302.9 6.2 %copy.62 = bf16[16,2,32,3072]{3,2,1,0:T(8,128)(2,1)} copy(bf16[16,2,32,3072]{3,2,0,1:T(8,128)(2,1)} %bitcast.71) | data formatting | bytes 12582912 | tf_op jit(solution)/shard_map/transpose | solution.py:299
  309.1 46.6 %all-gather.4.cloned.1.call-done = f32[32,72,128]{2,1,0:T(8,128)} async-done(((f32[1,72,128]{2,1,0:T(8,128)}), f32[32,72,128]{2,1,0:T(8,128)}) %all-gather.4.cloned.1.call-update) | async-done | bytes 1179664 | tf_op jit(solution)/shard_map/all_gather | solution.py:311
  355.7 1.3 reduce_sum.9
  357.3 0.7 reshape.441
  362.7 112.2 %reduce-scatter.2.cloned.1.call-done = bf16[32,3072]{1,0:T(8,128)(2,1)} async-done(((bf16[1024,3072]{1,0:T(8,128)(2,1)}), bf16[32,3072]{1,0:T(8,128)(2,1)}) %reduce-scatter.2.cloned.1.call-update) | async-done | bytes 196624 | tf_op jit(solution)/shard_map/reduce_scatter | solution.py:300
  474.9 1.0 convert_element_type.55
  475.9 0.7 slice_bitcast_fusion
  476.6 0.6 slice_bitcast_fusion.2
  477.2 0.8 slice.138
  478.3 1.0 reshape.434
  479.3 0.7 slice.143
  (61 shorter events, 8.8 us)
Async XLA Ops:
  7.2 11.0 %copy-start = (bf16[16,169]{1,0:T(8,128)(2,1)S(1)}, bf16[16,169]{1,0:T(8,128)(2,1)}, u32[]{:S(2)}) copy-start(bf16[16,169]{1,0:T(8,128)(2,1)} %param.30) | copy-start | bytes 16228
  7.2 83.5 %all-gather.6.cloned.1.call-start = ((), (), s32[]{:S(2)}) async-start(), calls=%async_computation.3 | async-start | bytes 6758400 | tf_op jit(solution)/shard_map/all_gather | solution.py:275
  16.4 0.7 copy-start.2
  17.1 338.6 %all-gather.4.cloned.1.call-start = ((), (), s32[]{:S(2)}) async-start(), calls=%async_computation.2 | async-start | bytes 1216512 | tf_op jit(solution)/shard_map/all_gather | solution.py:311
  302.9 172.0 %reduce-scatter.2.cloned.1.call-start = ((), (), s32[]{:S(2)}) async-start(), calls=%async_computation.1 | async-start | bytes 6488064 | tf_op jit(solution)/shard_map/reduce_scatter | solution.py:300
  474.9 4.4 copy-start.1
Sparse Core Ops, SparseCore 0:
  17.2 73.3 all-gather.5
  303.0 52.6 all-gather.3
  361.3 113.5 reduce-scatter.1
